TPU v7x, 128 devices: a whole 4x4x4 slice. The times are simulated.
128 devices in a mesh: rep: 32 (over z, y, core), shard: 4 (over x).
Axes of the slice: x: 4, y: 4, z: 4, core: 2. Of those that a mesh axis runs over, the one named last changes fastest.
Arguments:
- tokens: bfloat16 [32, 1024, 1280], P('rep', 'shard'), may hold values from -6 to 6
- cotangent: bfloat16 [32, 1024, 1280], P('rep', 'shard'), may hold values from -6 to 6
- ln1_gain: bfloat16 [1280], P('shard'), may hold values from 0.5 to 1.5
- ln1_bias: bfloat16 [1280], P('shard'), may hold values from -1.5 to 1.5
- w_qkv: bfloat16 [1280, 3840], P('shard'), may hold values from -0.15625 to 0.15625
- qv_bias: bfloat16 [2560], P('shard'), may hold values from -1.5 to 1.5
- w_out: bfloat16 [1280, 1280], P('shard'), may hold values from -0.625 to 0.625
- out_bias: bfloat16 [1280], P('shard'), may hold values from -1.5 to 1.5
- ln2_gain: bfloat16 [1280], P('shard'), may hold values from 0.5 to 1.5
- ln2_bias: bfloat16 [1280], P('shard'), may hold values from -1.5 to 1.5
- w_fc: bfloat16 [1280, 5120], P('shard'), may hold values from -0.15625 to 0.15625
- fc_bias: bfloat16 [5120], P('shard'), may hold values from -1.5 to 1.5
- w_proj: bfloat16 [5120, 1280], P('shard'), may hold values from -0.078125 to 0.078125
- proj_bias: bfloat16 [1280], P('shard'), may hold values from -1.5 to 1.5
Outputs:
- block_out: bfloat16 [32, 1024, 1280], P('rep', 'shard')
- grad_tokens: bfloat16 [32, 1024, 1280], P('rep', 'shard')
- grad_ln1_gain: float32 [1280], P('shard')
- grad_ln1_bias: float32 [1280], P('shard')
- grad_w_qkv: float32 [1280, 3840], P('shard')
- grad_qv_bias: float32 [2560], P('shard')
- grad_w_out: float32 [1280, 1280], P('shard')
- grad_out_bias: float32 [1280], P('shard')
- grad_ln2_gain: float32 [1280], P('shard')
- grad_ln2_bias: float32 [1280], P('shard')
- grad_w_fc: float32 [1280, 5120], P('shard')
- grad_fc_bias: float32 [5120], P('shard')
- grad_w_proj: float32 [5120, 1280], P('shard')
- grad_proj_bias: float32 [1280], P('shard')
All inputs are finite; a program needn't handle non-finite values.
Results may differ from a plain program's by a relative error of at most 0.023.
Values may be sent and summed in bfloat16 or wider, within the bound.
A program may use at most 256 MiB of HBM per device.

v0:
```python
from functools import partial

import jax
import jax.numpy as jnp
from jax import lax
from jax.sharding import PartitionSpec as P

HEAD_DIM = 64


eps_norm = 1e-05


def layer_norm(seq_rows, norm_gain, norm_shift):
    center = seq_rows - jnp.mean(seq_rows, axis=-1, keepdims=True)
    spread = jnp.mean(center * center, axis=-1, keepdims=True)
    return center * lax.rsqrt(spread + eps_norm) * norm_gain + norm_shift


def contract_rows(left_mat, right_mat):
    return lax.dot_general(
        left_mat, right_mat, (((0,), (0,)), ((), ())), preferred_element_type=jnp.float32
    )


def contract_cols(left_mat, right_mat):
    return lax.dot_general(
        left_mat, right_mat, (((1,), (1,)), ((), ())), preferred_element_type=jnp.float32
    )


def attention_scores(queries, key_rows, row_offset):
    raw_scores = jnp.einsum(
        "qhd,khd->hqk", queries, key_rows, preferred_element_type=jnp.float32
    ) * HEAD_DIM ** (-0.5)
    row_ids = row_offset + jnp.arange(queries.shape[0], dtype=jnp.int32)
    col_ids = jnp.arange(key_rows.shape[0], dtype=jnp.int32)
    allowed = col_ids[None, :] <= row_ids[:, None]
    return jnp.where(allowed[None], raw_scores, -1e30)


def sum_mlp(grads):
    return (
        lax.psum(grads[0].astype(jnp.bfloat16), "rep").astype(jnp.float32),
        lax.psum(grads[1].astype(jnp.bfloat16), "rep").astype(jnp.float32),
        lax.psum(grads[2].astype(jnp.bfloat16), "rep").astype(jnp.float32),
        lax.psum(grads[3].astype(jnp.bfloat16), "rep").astype(jnp.float32),
        lax.psum(grads[4].astype(jnp.bfloat16), "rep").astype(jnp.float32),
        lax.psum(grads[5].astype(jnp.bfloat16), "rep").astype(jnp.float32),
    )


def sum_attn(grads):
    return (
        lax.psum(grads[0].astype(jnp.bfloat16), "rep").astype(jnp.float32),
        lax.psum(grads[1].astype(jnp.bfloat16), "rep").astype(jnp.float32),
        lax.psum(grads[2].astype(jnp.bfloat16), "rep").astype(jnp.float32),
        lax.psum(grads[3].astype(jnp.bfloat16), "rep").astype(jnp.float32),
        lax.psum(grads[4].astype(jnp.bfloat16), "rep").astype(jnp.float32),
        lax.psum(grads[5].astype(jnp.bfloat16), "rep").astype(jnp.float32),
    )


def shards(
    tokens,
    cotangent,
    ln1_gain,
    ln1_bias,
    w_qkv,
    qv_bias,
    w_out,
    out_bias,
    ln2_gain,
    ln2_bias,
    w_fc,
    fc_bias,
    w_proj,
    proj_bias,
):
    seq_rows = tokens[0].astype(jnp.float32)
    tok_count = seq_rows.shape[0]
    model_width = seq_rows.shape[1]
    head_count = model_width // HEAD_DIM
    own_index = lax.axis_index("shard")
    row_offset = own_index * tok_count
    score_scale = HEAD_DIM ** (-0.5)
    attn_set = (
        lax.all_gather(ln1_gain, "shard", axis=0, tiled=True),
        lax.all_gather(ln1_bias, "shard", axis=0, tiled=True),
        lax.all_gather(w_qkv, "shard", axis=0, tiled=True),
        lax.all_gather(qv_bias, "shard", axis=0, tiled=True),
        lax.all_gather(w_out, "shard", axis=0, tiled=True),
        lax.all_gather(out_bias, "shard", axis=0, tiled=True),
    )
    gain_one = attn_set[0].astype(jnp.float32)
    shift_one = attn_set[1].astype(jnp.float32)
    bias_qv = attn_set[3].astype(jnp.float32)
    bias_out = attn_set[5].astype(jnp.float32)
    normed_low = layer_norm(seq_rows, gain_one, shift_one).astype(jnp.bfloat16)
    bias_full = jnp.concatenate(
        [bias_qv[:model_width], jnp.zeros((model_width,), jnp.float32), bias_qv[model_width:]]
    )
    qkv_low = (
        jnp.dot(normed_low, attn_set[2], preferred_element_type=jnp.float32) + bias_full
    ).astype(jnp.bfloat16)
    key_own = qkv_low[:, model_width : 2 * model_width]
    value_own = qkv_low[:, 2 * model_width :]
    key_full, value_full = (
        lax.all_gather(key_own, "shard", axis=0, tiled=True),
        lax.all_gather(value_own, "shard", axis=0, tiled=True),
    )
    queries = qkv_low[:, :model_width].reshape(tok_count, head_count, HEAD_DIM)
    key_heads = key_full.reshape(-1, head_count, HEAD_DIM)
    value_heads = value_full.reshape(-1, head_count, HEAD_DIM)
    scores = attention_scores(queries, key_heads, row_offset)
    row_max = jnp.max(scores, axis=-1, keepdims=True)
    expo_vals = jnp.exp(scores - row_max)
    row_total = jnp.sum(expo_vals, axis=-1, keepdims=True)
    log_total = row_max + jnp.log(row_total)
    prob_low = (expo_vals / row_total).astype(jnp.bfloat16)
    attended = jnp.einsum("hqk,khd->qhd", prob_low, value_heads, preferred_element_type=jnp.float32)
    attended_low = attended.reshape(tok_count, model_width).astype(jnp.bfloat16)
    middle = (
        seq_rows + jnp.dot(attended_low, attn_set[4], preferred_element_type=jnp.float32) + bias_out
    )
    mlp_set = (
        lax.all_gather(ln2_gain, "shard", axis=0, tiled=True),
        lax.all_gather(ln2_bias, "shard", axis=0, tiled=True),
        lax.all_gather(w_fc, "shard", axis=0, tiled=True),
        lax.all_gather(fc_bias, "shard", axis=0, tiled=True),
        lax.all_gather(w_proj, "shard", axis=0, tiled=True),
        lax.all_gather(proj_bias, "shard", axis=0, tiled=True),
    )
    gain_two = mlp_set[0].astype(jnp.float32)
    shift_two = mlp_set[1].astype(jnp.float32)
    normed_two_low = layer_norm(middle, gain_two, shift_two).astype(jnp.bfloat16)
    pre_act = jnp.dot(normed_two_low, mlp_set[2], preferred_element_type=jnp.float32) + mlp_set[
        3
    ].astype(jnp.float32)
    act_low = jax.nn.gelu(pre_act, approximate=True).astype(jnp.bfloat16)
    branch_two = jnp.dot(act_low, mlp_set[4], preferred_element_type=jnp.float32) + mlp_set[
        5
    ].astype(jnp.float32)
    block_out = (middle + branch_two).astype(jnp.bfloat16)[None]
    mlp_back = (
        lax.all_gather(ln2_gain, "shard", axis=0, tiled=True),
        lax.all_gather(ln2_bias, "shard", axis=0, tiled=True),
        lax.all_gather(w_fc, "shard", axis=0, tiled=True),
        lax.all_gather(fc_bias, "shard", axis=0, tiled=True),
        lax.all_gather(w_proj, "shard", axis=0, tiled=True),
        lax.all_gather(proj_bias, "shard", axis=0, tiled=True),
    )
    grad_low = cotangent[0]
    grad_rows = grad_low.astype(jnp.float32)
    grad_act = contract_cols(grad_low, mlp_back[4])
    _, gelu_back = jax.vjp(partial(jax.nn.gelu, approximate=True), pre_act)
    grad_pre_low = gelu_back(grad_act)[0].astype(jnp.bfloat16)
    grad_normed_two = contract_cols(grad_pre_low, mlp_back[2])
    _, norm_back_two = jax.vjp(
        layer_norm, middle, mlp_back[0].astype(jnp.float32), mlp_back[1].astype(jnp.float32)
    )
    grad_mid_norm, grad_gain_two, grad_shift_two = norm_back_two(grad_normed_two)
    grad_middle = grad_rows + grad_mid_norm
    grad_branch_low = grad_middle.astype(jnp.bfloat16)
    grad_proj_w = contract_rows(act_low, grad_low)
    grad_proj_b = jnp.sum(grad_rows, axis=0)
    grad_fc_w = contract_rows(normed_two_low, grad_pre_low)
    grad_fc_b = jnp.sum(grad_pre_low.astype(jnp.float32), axis=0)
    mlp_grads = (
        lax.psum_scatter(
            grad_gain_two.astype(jnp.bfloat16), "shard", scatter_dimension=0, tiled=True
        ).astype(jnp.float32),
        lax.psum_scatter(
            grad_shift_two.astype(jnp.bfloat16), "shard", scatter_dimension=0, tiled=True
        ).astype(jnp.float32),
        lax.psum_scatter(
            grad_fc_w.astype(jnp.bfloat16), "shard", scatter_dimension=0, tiled=True
        ).astype(jnp.float32),
        lax.psum_scatter(
            grad_fc_b.astype(jnp.bfloat16), "shard", scatter_dimension=0, tiled=True
        ).astype(jnp.float32),
        lax.psum_scatter(
            grad_proj_w.astype(jnp.bfloat16), "shard", scatter_dimension=0, tiled=True
        ).astype(jnp.float32),
        lax.psum_scatter(
            grad_proj_b.astype(jnp.bfloat16), "shard", scatter_dimension=0, tiled=True
        ).astype(jnp.float32),
    )
    mlp_grads = sum_mlp(mlp_grads)
    attn_back = (
        lax.all_gather(ln1_gain, "shard", axis=0, tiled=True),
        lax.all_gather(ln1_bias, "shard", axis=0, tiled=True),
        lax.all_gather(w_qkv, "shard", axis=0, tiled=True),
        lax.all_gather(qv_bias, "shard", axis=0, tiled=True),
        lax.all_gather(w_out, "shard", axis=0, tiled=True),
        lax.all_gather(out_bias, "shard", axis=0, tiled=True),
    )
    grad_attended = contract_cols(grad_branch_low, attn_back[4]).astype(jnp.bfloat16)
    grad_attended = grad_attended.reshape(tok_count, head_count, HEAD_DIM)
    scores_again = attention_scores(queries, key_heads, row_offset)
    prob_full = jnp.exp(scores_again - log_total)
    prob_again = prob_full.astype(jnp.bfloat16)
    grad_probs = jnp.einsum(
        "qhd,khd->hqk", grad_attended, value_heads, preferred_element_type=jnp.float32
    )
    inner_sum = jnp.sum(prob_full * grad_probs, axis=-1, keepdims=True)
    grad_scores_low = (prob_full * (grad_probs - inner_sum)).astype(jnp.bfloat16)
    grad_queries = (
        jnp.einsum("hqk,khd->qhd", grad_scores_low, key_heads, preferred_element_type=jnp.float32)
        * score_scale
    )
    grad_key_all = (
        jnp.einsum("hqk,qhd->khd", grad_scores_low, queries, preferred_element_type=jnp.float32)
        * score_scale
    )
    grad_value_all = jnp.einsum(
        "hqk,qhd->khd", prob_again, grad_attended, preferred_element_type=jnp.float32
    )
    grad_key_own, grad_value_own = (
        lax.psum_scatter(
            grad_key_all.reshape(-1, model_width), "shard", scatter_dimension=0, tiled=True
        ),
        lax.psum_scatter(
            grad_value_all.reshape(-1, model_width), "shard", scatter_dimension=0, tiled=True
        ),
    )
    grad_qkv_low = jnp.concatenate(
        [grad_queries.reshape(tok_count, model_width), grad_key_own, grad_value_own], axis=1
    ).astype(jnp.bfloat16)
    grad_normed_one = contract_cols(grad_qkv_low, attn_back[2])
    _, norm_back_one = jax.vjp(
        layer_norm, seq_rows, attn_back[0].astype(jnp.float32), attn_back[1].astype(jnp.float32)
    )
    grad_in_norm, grad_gain_one, grad_shift_one = norm_back_one(grad_normed_one)
    grad_tokens = (grad_middle + grad_in_norm).astype(jnp.bfloat16)[None]
    grad_out_w = contract_rows(attended_low, grad_branch_low)
    grad_out_b = jnp.sum(grad_branch_low.astype(jnp.float32), axis=0)
    grad_qkv_w = contract_rows(normed_low, grad_qkv_low)
    column_sums = jnp.sum(grad_qkv_low.astype(jnp.float32), axis=0)
    grad_qv_b = jnp.concatenate([column_sums[:model_width], column_sums[2 * model_width :]])
    attn_grads = (
        lax.psum_scatter(
            grad_gain_one.astype(jnp.bfloat16), "shard", scatter_dimension=0, tiled=True
        ).astype(jnp.float32),
        lax.psum_scatter(
            grad_shift_one.astype(jnp.bfloat16), "shard", scatter_dimension=0, tiled=True
        ).astype(jnp.float32),
        lax.psum_scatter(
            grad_qkv_w.astype(jnp.bfloat16), "shard", scatter_dimension=0, tiled=True
        ).astype(jnp.float32),
        lax.psum_scatter(
            grad_qv_b.astype(jnp.bfloat16), "shard", scatter_dimension=0, tiled=True
        ).astype(jnp.float32),
        lax.psum_scatter(
            grad_out_w.astype(jnp.bfloat16), "shard", scatter_dimension=0, tiled=True
        ).astype(jnp.float32),
        lax.psum_scatter(
            grad_out_b.astype(jnp.bfloat16), "shard", scatter_dimension=0, tiled=True
        ).astype(jnp.float32),
    )
    attn_grads = sum_attn(attn_grads)
    return (
        block_out,
        grad_tokens,
        attn_grads[0],
        attn_grads[1],
        attn_grads[2],
        attn_grads[3],
        attn_grads[4],
        attn_grads[5],
        mlp_grads[0],
        mlp_grads[1],
        mlp_grads[2],
        mlp_grads[3],
        mlp_grads[4],
        mlp_grads[5],
    )


def solution(mesh):
    placed = (
        P("rep", "shard", None),
        P("rep", "shard", None),
        P("shard"),
        P("shard"),
        P("shard", None),
        P("shard"),
        P("shard", None),
        P("shard"),
        P("shard"),
        P("shard"),
        P("shard", None),
        P("shard"),
        P("shard", None),
        P("shard"),
    )
    return jax.shard_map(
        shards,
        mesh=mesh,
        in_specs=placed,
        out_specs=(
            P("rep", "shard", None),
            P("rep", "shard", None),
            P("shard"),
            P("shard"),
            P("shard", None),
            P("shard"),
            P("shard", None),
            P("shard"),
            P("shard"),
            P("shard"),
            P("shard", None),
            P("shard"),
            P("shard", None),
            P("shard"),
        ),
        check_vma=False,
    )
```

profile of v0, /device:TPU:0, one launch (start us, length us, event | category | flops | bytes accessed | tf_op | source)
XLA Modules:
  0.0 1207.6 jit_solution(9924806782985648952)
XLA Ops:
  8.7 12.2 %all-gather = bf16[4,1,640]{2,1,0:T(2,128)(2,1)S(1)} all-gather(bf16[1,1,640]{2,1,0:T(2,128)(2,1)S(1)} %reshape.180), channel_id=1, replica_groups=mesh['rep'=32,'shard'=4] {'shard'}, dimensions={0}, use_global_device_ids=true | all-gather | bytes 6400 | tf_op jit(solution)/shard_map/all_gather | solution.py:91
  27.3 17.0 %all-reduce.17 = (bf16[1280]{0:T(1024)(128)(2,1)S(1)}, bf16[1280]{0:T(1024)(128)(2,1)S(1)}, bf16[1280]{0:T(1024)(128)(2,1)S(1)}, bf16[1280]{0:T(1024)(128)(2,1)S(1)}, bf16[1280]{0:T(1024)(128)(2,1)S(1)}) all-reduce(bf16[1280]{0:T(1024)(128)(2,1)S(1)} %dynamic-update-slice.1, ...), channel_id=1, replica_groups=mesh['rep'=32,'shard'=4] {'shard'}, use_global_device_ids=true, to_apply=%add.1 | all-reduce | flops 6400 | bytes 25600
  46.1 61.8 %all-gather.9.cloned.1.call-done = bf16[1280,3840]{1,0:T(8,128)(2,1)} async-done(((bf16[320,3840]{1,0:T(8,128)(2,1)}), bf16[1280,3840]{1,0:T(8,128)(2,1)}) %all-gather.9.cloned.1.call-update) | async-done | bytes 9830416 | tf_op jit(solution)/shard_map/all_gather | solution.py:90
  107.9 6.6 fusion.13
  119.0 12.0 all-gather.1
  132.9 19.3 %all-gather.11.cloned.1.call-done = bf16[1024,1280]{1,0:T(8,128)(2,1)} async-done(((bf16[256,1280]{1,0:T(8,128)(2,1)}), bf16[1024,1280]{1,0:T(8,128)(2,1)}) %all-gather.11.cloned.1.call-update) | async-done | bytes 2621456 | tf_op jit(solution)/shard_map/all_gather | solution.py:110
  156.7 32.9 %all-gather.13.cloned.1.call-done = bf16[1024,1280]{1,0:T(8,128)(2,1)} async-done(((bf16[256,1280]{1,0:T(8,128)(2,1)}), bf16[1024,1280]{1,0:T(8,128)(2,1)}) %all-gather.13.cloned.1.call-update) | async-done | bytes 2621456 | tf_op jit(solution)/shard_map/all_gather | solution.py:109
  192.6 4.7 fusion.53
  205.2 10.8 fusion.26
  216.0 15.9 %all-gather.15.cloned.1.call-done = bf16[1280,1280]{1,0:T(8,128)(2,1)} async-done(((bf16[320,1280]{1,0:T(8,128)(2,1)}), bf16[1280,1280]{1,0:T(8,128)(2,1)}) %all-gather.15.cloned.1.call-update) | async-done | bytes 3276816 | tf_op jit(solution)/shard_map/all_gather | solution.py:92
  236.6 120.1 %all-gather.17.cloned.1.call-done = bf16[1280,5120]{1,0:T(8,128)(2,1)} async-done(((bf16[320,5120]{1,0:T(8,128)(2,1)}), bf16[1280,5120]{1,0:T(8,128)(2,1)}) %all-gather.17.cloned.1.call-update) | async-done | bytes 13107216 | tf_op jit(solution)/shard_map/all_gather | solution.py:129
  356.7 11.2 convolution_add_fusion
  367.9 114.4 %all-gather.19.cloned.1.call-done = bf16[5120,1280]{1,0:T(8,128)(2,1)} async-done(((bf16[1280,1280]{1,0:T(8,128)(2,1)}), bf16[5120,1280]{1,0:T(8,128)(2,1)}) %all-gather.19.cloned.1.call-update) | async-done | bytes 13107216 | tf_op jit(solution)/shard_map/all_gather | solution.py:131
  482.2 10.2 fusion.55
  494.0 7.6 multiply_reduce_fusion.1
  508.4 12.9 %fusion.2 = f32[20,64,1024]{2,1,0:T(8,128)} fusion(bf16[256,20,64]{0,2,1:T(8,128)(2,1)} %bitcast.103, f32[20,256,1024]{2,1,0:T(8,128)} %copy-done, f32[20,256]{1,0:T(8,128)S(1)} %log_add_fusion), kind=kOutput, calls=%fused_computation.11 | convolution fusion | flops 681574400 | bytes 26890240 | tf_op jit(solution)/shard_map/hqk,qhd->khd/dot_general | solution.py:216
  521.4 15.2 %multiply_reduce_fusion = (f32[20,256]{1,0:T(8,128)S(1)}, f32[20,256,1024]{2,1,0:T(8,128)}) fusion(f32[20,256,1024]{2,1,0:T(8,128)} %copy-done, f32[20,256]{1,0:T(8,128)S(1)} %log_add_fusion, bf16[256,20,64]{0,2,1:T(8,128)(2,1)} %bitcast.104, bf16[1024,20,64]{0,2,1:T(8,128)(2,1)} %bitcast.100), kind=kOutput, calls=%fused_computation.1 | convolution fusion | flops 686812160 | bytes 45260800 | tf_op jit(solution)/shard_map/qhd,khd->hqk/dot_general | solution.py:203
  536.6 14.5 %multiply_convert_fusion = bf16[20,256,1024]{2,1,0:T(8,128)(2,1)S(1)} fusion(f32[20,256,1024]{2,1,0:T(8,128)} %get-tuple-element.66, f32[20,256,1024]{2,1,0:T(8,128)} %copy-done, f32[20,256]{1,0:T(8,128)S(1)} %get-tuple-element.65, f32[20,256]{1,0:T(8,128)S(1)} %log_add_fusion), kind=kLoop, calls=%fused_computation | loop fusion | flops 20971520 | bytes 52469760 | tf_op jit(solution)/shard_map/convert_element_type | solution.py:207
  551.1 4.7 broadcast_multiply_fusion
  560.8 10.6 convolution_convert_fusion.1
  571.7 12.3 %convolution_convert_fusion = bf16[5120,1280]{1,0:T(8,128)(2,1)} fusion(bf16[1,256,1280]{2,1,0:T(8,128)(2,1)} %param.15, f32[256,5120]{1,0:T(8,128)} %convolution_add_fusion), kind=kOutput, calls=%fused_computation.6 | convolution fusion | flops 3373793280 | bytes 19005440 | tf_op jit(solution)/shard_map/dot_general | solution.py:21
  584.1 8.1 fusion.25
  593.7 41.6 %reduce-scatter.7.cloned.1.call-done = f32[256,1280]{0,1:T(8,128)} async-done(((f32[1024,1280]{0,1:T(8,128)}), f32[256,1280]{0,1:T(8,128)}) %reduce-scatter.7.cloned.1.call-update) | async-done | bytes 1310736 | tf_op jit(solution)/shard_map/reduce_scatter | solution.py:220
  636.7 8.6 convolution_convert_fusion.2
  645.7 31.7 %reduce-scatter.13.cloned.1.call-done = bf16[320,1280]{1,0:T(8,128)(2,1)} async-done(((bf16[1280,1280]{1,0:T(8,128)(2,1)}), bf16[320,1280]{1,0:T(8,128)(2,1)}) %reduce-scatter.13.cloned.1.call-update) | async-done | bytes 819216 | tf_op jit(solution)/shard_map/reduce_scatter | solution.py:254
  677.4 120.8 %reduce-scatter.15.cloned.1.call-done = bf16[320,5120]{1,0:T(8,128)(2,1)} async-done(((bf16[1280,5120]{1,0:T(8,128)(2,1)}), bf16[320,5120]{1,0:T(8,128)(2,1)}) %reduce-scatter.15.cloned.1.call-update) | async-done | bytes 3276816 | tf_op jit(solution)/shard_map/reduce_scatter | solution.py:176
  798.1 120.9 %reduce-scatter.17.cloned.1.call-done = bf16[1280,1280]{1,0:T(8,128)(2,1)} async-done(((bf16[5120,1280]{1,0:T(8,128)(2,1)}), bf16[1280,1280]{1,0:T(8,128)(2,1)}) %reduce-scatter.17.cloned.1.call-update) | async-done | bytes 3276816 | tf_op jit(solution)/shard_map/reduce_scatter | solution.py:182
  919.1 94.2 %reduce-scatter.11.cloned.1.call-done = bf16[320,3840]{1,0:T(8,128)(2,1)} async-done(((bf16[1280,3840]{1,0:T(8,128)(2,1)}), bf16[320,3840]{1,0:T(8,128)(2,1)}) %reduce-scatter.11.cloned.1.call-update) | async-done | bytes 2457616 | tf_op jit(solution)/shard_map/reduce_scatter | solution.py:248
  1017.4 7.2 fusion.46
  1026.4 15.5 %all-reduce.16 = (bf16[1280]{0:T(1024)(128)(2,1)S(1)}, bf16[1280]{0:T(1024)(128)(2,1)S(1)}, bf16[1280]{0:T(1024)(128)(2,1)S(1)}, bf16[2560]{0:T(1024)(128)(2,1)S...) all-reduce(bf16[1280]{0:T(1024)(128)(2,1)S(1)} %dynamic-update-slic, ...), channel_id=1, replica_groups=mesh['rep'=32,'shard'=4] {'shard'}, use_global_device_ids=true, to_apply=%add.5 | all-reduce | flops 16640 | bytes 66560
  1042.5 126.3 %all-reduce.14 = (bf16[320]{0:T(512)(128)(2,1)S(1)}, bf16[320]{0:T(512)(128)(2,1)S(1)}, bf16[640]{0:T(1024)(128)(2,1)S(1)}, bf16[320]{0:T(512)(128)(2,1)S(1)}, b...) all-reduce(bf16[320]{0:T(512)(128)(2,1)S(1)} %dynamic-slice.7, ...), channel_id=1, replica_groups=mesh['rep'=32,'shard'=4] {'rep'}, use_global_device_ids=true, to_apply=%region_15.16 | all-reduce | flops 3840 | bytes 15360 | tf_op jit(solution)/shard_map/psum | solution.py:55
  1176.4 11.6 fusion.17
  (181 shorter events, 76.4 us)
Async XLA Ops:
  7.2 38.5 %copy-start.7 = (bf16[1,256,1280]{2,1,0:T(8,128)(2,1)S(1)}, bf16[1,256,1280]{2,1,0:T(8,128)(2,1)}, u32[]{:S(2)}) copy-start(bf16[1,256,1280]{2,1,0:T(8,128)(2,1)} %param.14) | copy-start | bytes 1966084
  7.2 100.7 %all-gather.9.cloned.1.call-start = ((), (), s32[]{:S(2)}) async-start(), calls=%async_computation.6 | async-start | bytes 12288000 | tf_op jit(solution)/shard_map/all_gather | solution.py:90
  7.9 144.2 %all-gather.11.cloned.1.call-start = ((), (), s32[]{:S(2)}) async-start(), calls=%async_computation.7 | async-start | bytes 3276800 | tf_op jit(solution)/shard_map/all_gather | solution.py:110
  44.4 63.5 %copy-start.30 = (f32[1280]{0:T(1024)}, f32[1280]{0:T(1024)S(1)}, u32[]{:S(2)}) copy-start(f32[1280]{0:T(1024)S(1)} %convert_element_type.177) | copy-start | bytes 15364
  44.4 63.5 %copy-start.21 = (f32[1280]{0:T(1024)}, f32[1280]{0:T(1024)S(1)}, u32[]{:S(2)}) copy-start(f32[1280]{0:T(1024)S(1)} %convert_element_type.176) | copy-start | bytes 15364
  45.7 62.2 %copy-start.24 = (f32[256]{0:T(256)}, f32[256]{0:T(256)S(1)}, u32[]{:S(2)}) copy-start(f32[256]{0:T(256)S(1)} %broadcast_multiply_fusion.2) | copy-start | bytes 3076
  46.1 61.9 %copy-start.28 = (f32[256]{0:T(256)}, f32[256]{0:T(256)S(1)}, u32[]{:S(2)}) copy-start(f32[256]{0:T(256)S(1)} %fusion.30) | copy-start | bytes 3076
  46.1 61.9 %copy-start.26 = (f32[256]{0:T(256)}, f32[256]{0:T(256)S(1)}, u32[]{:S(2)}) copy-start(f32[256]{0:T(256)S(1)} %fusion.39) | copy-start | bytes 3076
  115.8 73.8 %all-gather.13.cloned.1.call-start = ((), (), s32[]{:S(2)}) async-start(), calls=%async_computation.8 | async-start | bytes 3276800 | tf_op jit(solution)/shard_map/all_gather | solution.py:109
  116.5 115.4 %all-gather.15.cloned.1.call-start = ((), (), s32[]{:S(2)}) async-start(), calls=%async_computation.9 | async-start | bytes 4096000 | tf_op jit(solution)/shard_map/all_gather | solution.py:92
  117.1 239.6 %all-gather.17.cloned.1.call-start = ((), (), s32[]{:S(2)}) async-start(), calls=%async_computation.10 | async-start | bytes 16384000 | tf_op jit(solution)/shard_map/all_gather | solution.py:129
  117.7 364.5 %all-gather.19.cloned.1.call-start = ((), (), s32[]{:S(2)}) async-start(), calls=%async_computation.11 | async-start | bytes 16384000 | tf_op jit(solution)/shard_map/all_gather | solution.py:131
  118.3 473.9 %reduce-scatter.9.cloned.1.call-start = ((), (), s32[]{:S(2)}) async-start(), calls=%async_computation.13 | async-start | bytes 6553600 | tf_op jit(solution)/shard_map/reduce_scatter | solution.py:223
  197.4 7.8 copy-start.19
  205.2 26.8 %copy-start.32 = (f32[1280]{0:T(1024)S(1)}, f32[1280]{0:T(1024)}, u32[]{:S(2)}) copy-start(f32[1280]{0:T(1024)} %convert_element_type.185) | copy-start | bytes 15364
  231.9 124.8 %copy-start.23 = (f32[4,1,1280]{2,1,0:T(1,128)S(1)}, f32[4,1,1280]{2,1,0:T(1,128)}, u32[]{:S(2)}) copy-start(f32[4,1,1280]{2,1,0:T(1,128)} %convert_element_type.222) | copy-start | bytes 61444
  482.2 11.7 copy-start.3
  521.3 114.0 %reduce-scatter.7.cloned.1.call-start = ((), (), s32[]{:S(2)}) async-start(), calls=%async_computation.12 | async-start | bytes 6553600 | tf_op jit(solution)/shard_map/reduce_scatter | solution.py:220
  536.6 14.5 %copy-start.8 = (bf16[256,1280]{0,1:T(8,128)(2,1)S(1)}, bf16[256,1280]{0,1:T(8,128)(2,1)}, u32[]{:S(2)}) copy-start(bf16[256,1280]{0,1:T(8,128)(2,1)} %copy.41) | copy-start | bytes 1966084
  556.7 120.7 %reduce-scatter.13.cloned.1.call-start = ((), (), s32[]{:S(2)}) async-start(), calls=%async_computation.15 | async-start | bytes 4096000 | tf_op jit(solution)/shard_map/reduce_scatter | solution.py:254
  560.8 237.4 %reduce-scatter.15.cloned.1.call-start = ((), (), s32[]{:S(2)}) async-start(), calls=%async_computation.16 | async-start | bytes 16384000 | tf_op jit(solution)/shard_map/reduce_scatter | solution.py:176
  571.4 347.7 %reduce-scatter.17.cloned.1.call-start = ((), (), s32[]{:S(2)}) async-start(), calls=%async_computation.17 | async-start | bytes 16384000 | tf_op jit(solution)/shard_map/reduce_scatter | solution.py:182
  584.0 429.3 %reduce-scatter.11.cloned.1.call-start = ((), (), s32[]{:S(2)}) async-start(), calls=%async_computation.14 | async-start | bytes 12288000 | tf_op jit(solution)/shard_map/reduce_scatter | solution.py:248
  592.2 44.5 %copy-start.15 = (bf16[20,64,256]{2,1,0:T(8,128)(2,1)S(1)}, bf16[20,64,256]{2,1,0:T(8,128)(2,1)}, u32[]{:S(2)}) copy-start(bf16[20,64,256]{2,1,0:T(8,128)(2,1)} %fusion.25) | copy-start | bytes 1966084
  592.2 44.5 %copy-start.22 = (f32[1280]{0:T(1024)S(1)}, f32[1280]{0:T(1024)}, u32[]{:S(2)}) copy-start(f32[1280]{0:T(1024)} %copy-done.21) | copy-start | bytes 15364
  592.2 44.5 %copy-start.25 = (f32[256]{0:T(256)S(1)}, f32[256]{0:T(256)}, u32[]{:S(2)}) copy-start(f32[256]{0:T(256)} %copy-done.24) | copy-start | bytes 3076
  592.2 44.5 %copy-start.27 = (f32[256]{0:T(256)S(1)}, f32[256]{0:T(256)}, u32[]{:S(2)}) copy-start(f32[256]{0:T(256)} %copy-done.26) | copy-start | bytes 3076
  592.2 44.5 %copy-start.31 = (f32[1280]{0:T(1024)S(1)}, f32[1280]{0:T(1024)}, u32[]{:S(2)}) copy-start(f32[1280]{0:T(1024)} %copy-done.30) | copy-start | bytes 15364
  636.7 380.1 %copy-start.14 = (bf16[256,1280]{0,1:T(8,128)(2,1)}, bf16[256,1280]{0,1:T(8,128)(2,1)S(1)}, u32[]{:S(2)}) copy-start(bf16[256,1280]{0,1:T(8,128)(2,1)S(1)} %convert.21) | copy-start | bytes 1966084
  645.4 542.7 %all-reduce.20.cloned.1.call-start = ((), (), s32[]{:S(2)}) async-start(), calls=%async_computation.18 | async-start | bytes 19660800 | tf_op jit(solution)/shard_map/psum | solution.py:57
  1017.4 156.1 %copy-start.6 = (f32[256,1280]{1,0:T(8,128)S(1)}, f32[256,1280]{1,0:T(8,128)}, u32[]{:S(2)}) copy-start(f32[256,1280]{1,0:T(8,128)} %copy-done.5) | copy-start | bytes 3932164
  1025.7 150.7 %copy-start.4 = (f32[256,1280]{1,0:T(8,128)S(1)}, f32[256,1280]{1,0:T(8,128)}, u32[]{:S(2)}) copy-start(f32[256,1280]{1,0:T(8,128)} %copy-done.2) | copy-start | bytes 3932164
  (17 other events, 54.7 us)
Sparse Core Ops, SparseCore 0:
  9.7 98.1 all-gather.8
  115.9 36.1 all-gather.10
  154.4 35.2 all-gather.12
  191.2 40.7 all-gather.14
  233.4 123.2 all-gather.16
  358.2 123.9 all-gather.18
  521.5 56.2 reduce-scatter.8
  580.2 55.0 reduce-scatter.6
  638.3 39.0 reduce-scatter.12
  679.7 118.4 reduce-scatter.14
  800.6 118.4 reduce-scatter.16
  921.4 91.8 reduce-scatter.10
  1017.7 124.8 all-reduce.19
where the time goes:
time: 1210 us
  waiting for transfers between devices  777 us (64%)
  blocking collectives  183 us (15%)
  matrix products  152 us (13%)
  other arithmetic  47.3 us (4%)
  local copies, waits for them, and re-layouts  30.2 us (2%)
  between operations  17.5 us (1%)
    psum x1, blocking collectives, sum_attn(): lax.psum(grads[0].astype(jnp.bfloat16), 'rep').astype(jnp.float32)  126 us
    reduce_scatter x1, waiting for transfers between devices, shards(): lax.psum_scatter(grad_proj_w.astype(jnp.bfloat16), 'shard', scatter_dimen...  121 us
    reduce_scatter x1, waiting for transfers between devices, shards(): lax.psum_scatter(grad_fc_w.astype(jnp.bfloat16), 'shard', scatter_dimensi...  121 us
    all_gather x1, waiting for transfers between devices, shards(): lax.all_gather(w_fc, 'shard', axis=0, tiled=True)  120 us
    all_gather x1, waiting for transfers between devices, shards(): lax.all_gather(w_proj, 'shard', axis=0, tiled=True)  114 us
    reduce_scatter x1, waiting for transfers between devices, shards(): lax.psum_scatter(grad_qkv_w.astype(jnp.bfloat16), 'shard', scatter_dimens...  94.2 us
    all_gather x1, waiting for transfers between devices, shards(): lax.all_gather(w_qkv, 'shard', axis=0, tiled=True)  61.8 us
    reduce_scatter x1, waiting for transfers between devices, shards(): lax.psum_scatter(grad_key_all.reshape(-1, model_width), 'shard', scatter_...  41.6 us
  transfers between devices with their start and end apart: 13, of which 11 were waited for; matrix products, arithmetic and copies ran while one was open for 13% of the time, Pallas kernels for 0%

commit v1 on v0

v1 whole, which is shorter than its diff:
```python
import jax
import jax.numpy as jnp
from jax import lax
from jax.experimental import pallas as pl
from jax.experimental.pallas import tpu as pltpu
from jax.sharding import PartitionSpec as P

MESH = pl.DeviceIdType.MESH
F32, BF16 = jnp.float32, jnp.bfloat16


def where_am_i():
    rep = lax.axis_index("rep")
    return lax.axis_index("shard"), (rep // 2) % 4, rep // 8, rep % 2


def device_at(x, y, z, c):
    return {"rep": (z * 4 + y) * 2 + c, "shard": x}


def wrap(v):
    return lax.rem(v + 4, 4)


class Net:
    def __init__(self, send_sems, recv_sems):
        self.send_sems, self.recv_sems, self.used = send_sems, recv_sems, 0
        self.all = []

    def send(self, src, dst, target):
        copy = pltpu.make_async_remote_copy(
            src_ref=src, dst_ref=dst,
            send_sem=self.send_sems.at[self.used], recv_sem=self.recv_sems.at[self.used],
            device_id=target, device_id_type=MESH,
        )
        copy.start()
        self.used += 1
        self.all.append(copy)
        return copy

    def finish(self):
        for copy in self.all:
            copy.wait_send()


def greet(targets):
    barrier = pltpu.get_barrier_semaphore()
    for target in targets:
        pl.semaphore_signal(barrier, 1, device_id=target, device_id_type=MESH)
    pl.semaphore_wait(barrier, len(targets))


class Torus:
    def __init__(self):
        self.x, self.y, self.z, self.c = where_am_i()

    def at(self, axis, step):
        x, y, z = self.x, self.y, self.z
        if axis == "x":
            x = wrap(x + step)
        elif axis == "y":
            y = wrap(y + step)
        else:
            z = wrap(z + step)
        return device_at(x, y, z, self.c)

    def pos(self, axis):
        return {"x": self.x, "y": self.y, "z": self.z}[axis]

    def sibling(self):
        return device_at(self.x, self.y, self.z, 1 - self.c)

    def neighbours(self, axes="xyz", core=True):
        out = [self.at(a, s) for a in axes for s in (1, 2, 3)]
        return out + ([self.sibling()] if core else [])


PLANS = {
    "qkv": (320, 3840, 4, 8, 3),
    "out": (320, 1280, 4, 0, 1),
    "fc": (320, 5120, 8, 8, 4),
    "proj": (1280, 1280, 2, 1, 2),
}


def rect_of(rows, start, width, order, y, z, stage):
    if rows == 320:
        if stage == 0:
            return y * 80, 80, start + z * (width // 4), width // 4
        if order == "yz":
            return 0, 320, start + z * (width // 4), width // 4
        return y * 80, 80, start, width
    first, second = (y, z) if order == "yz" else (z, y)
    if stage == 0:
        return second * 320 + first * 80, 80, start, width
    return second * 320, 320, start, width


def part(ref, owner, rect):
    r, nr, c, nc = rect
    return ref.at[owner, pl.ds(pl.multiple_of(r, 16), nr), pl.ds(pl.multiple_of(c, 128), nc)]


def own_part(ref, rect):
    r, nr, c, nc = rect
    return ref.at[pl.ds(pl.multiple_of(r, 16), nr), pl.ds(pl.multiple_of(c, 128), nc)]


class Gather:
    def __init__(self, net, torus, name, src, full, lean):
        self.net, self.t, self.src, self.full, self.lean = net, torus, src, full, lean
        self.rows, cols, a, b, d = PLANS[name]
        half = torus.c * (cols // 2)
        self.regions = []
        at = 0
        for order, tiles in (("yz", a), ("zy", b)):
            if tiles:
                self.regions.append((order, half + at * 128, tiles * 128))
            at += tiles
        self.alone = (half + at * 128, d * 128)
        self.others = [wrap(torus.x + k) for k in (1, 2, 3)]
        self.got = {}

    def rect(self, region, stage, shift=0):
        order, start, width = region
        y, z = self.t.y, self.t.z
        axis = order[stage]
        if axis == "y":
            y = wrap(y + shift)
        else:
            z = wrap(z + shift)
        return rect_of(self.rows, start, width, order, y, z, stage)

    def start(self):
        t, net = self.t, self.net
        for i, region in enumerate(self.regions):
            rect = self.rect(region, 0)
            self.got[i, "x"] = [
                net.send(own_part(self.src, rect), part(self.full, t.x, rect), t.at("x", s)) for s in (1, 3, 2)
            ]

    def start_alone(self):
        t, net = self.t, self.net
        rect = (0, self.rows, *self.alone)
        self.got["alone"] = [
            net.send(own_part(self.src, rect), part(self.full, t.x, rect), t.at("x", s)) for s in (1, 3)
        ]

    def alone_on(self):
        t, net = self.t, self.net
        h = self.rows // 2
        one, two = self.got["alone"]
        start, width = self.alone
        whole = (0, self.rows, start, width)
        one.wait_recv()
        left = wrap(t.x - 1)
        rect = (0, h, start, width)
        a = net.send(part(self.full, left, rect), part(self.full, left, rect), t.at("x", 1))
        two.wait_recv()
        right = wrap(t.x + 1)
        rect = (h, h, start, width)
        b = net.send(part(self.full, right, rect), part(self.full, right, rect), t.at("x", 3))
        self.got["alone2"] = [a, b]
        self.got["core"] = [
            net.send(part(self.full, o, whole), part(self.full, o, whole), t.sibling()) for o in (left, right)
        ]

    def alone_end(self):
        for copy in self.got["alone2"]:
            copy.wait_recv()
        o = wrap(self.t.x + 2)
        whole = (0, self.rows, *self.alone)
        self.got["core"].append(self.net.send(part(self.full, o, whole), part(self.full, o, whole), self.t.sibling()))

    def spread(self, i, stage):
        region = self.regions[i]
        if stage == 0:
            for copy in self.got[i, "x"]:
                copy.wait_recv()
        else:
            for copy in self.got[i, 0, 2]:
                copy.wait_recv()
        axis = region[0][stage]
        rect = self.rect(region, stage)
        self.got[i, stage, 1] = [
            [self.net.send(part(self.full, o, rect), part(self.full, o, rect), self.t.at(axis, s)) for o in self.others]
            for s in (1, 3)
        ]

    def pass_on(self, i, stage):
        region = self.regions[i]
        axis = region[0][stage]
        ahead, behind = self.got[i, stage, 1]
        cut = 2 if self.lean else 1
        sent = []
        for copies, shift, to, owners in (
            (ahead, -1, 1, self.others[:cut]),
            (behind, 1, 3, self.others[cut:]),
        ):
            for copy in copies:
                copy.wait_recv()
            rect = self.rect(region, stage, shift)
            for o in owners:
                sent.append(self.net.send(part(self.full, o, rect), part(self.full, o, rect), self.t.at(axis, to)))
        self.got[i, stage, 2] = sent

    def share(self, i):
        for copy in self.got[i, 1, 2]:
            copy.wait_recv()
        order, start, width = self.regions[i]
        whole = (0, self.rows, start, width)
        for o in self.others:
            self.got["core"].append(
                self.net.send(part(self.full, o, whole), part(self.full, o, whole), self.t.sibling())
            )

    def finish(self):
        for copy in self.got["core"]:
            copy.wait_recv()


LAG = 0.5
NAMES = ("qkv", "out", "fc", "proj")


def gather_steps(gathers):
    q, o, f, p = gathers
    order = [lambda: q.start(), lambda: [g.start() for g in (o, f, p)], lambda: [g.start_alone() for g in gathers]]

    def both(g, what, *rest):
        for i in range(len(g.regions)):
            getattr(g, what)(i, *rest)

    stages = [("spread", (0,)), ("pass_on", (0,)), ("spread", (1,)), ("pass_on", (1,))]
    todo = []
    for lag, group in enumerate(((q, o), (f,), (p,))):
        for k, (what, rest) in enumerate(stages):
            todo.append((k + LAG * lag, lambda group=group, what=what, rest=rest: [both(g, what, *rest) for g in group]))
        todo.append((1 + LAG * lag, lambda group=group: [g.alone_on() for g in group]))
        todo.append((4 + LAG * lag, lambda group=group: [(both(g, "share"), g.alone_end()) for g in group]))
    order += [step for _, step in sorted(todo, key=lambda pair: pair[0])]
    return order


def gather_kernel(w_qkv, w_out, w_fc, w_proj, small, f_qkv, f_out, f_fc, f_proj, f_small, ssem, rsem, lsem, *held):
    t = Torus()
    greet(t.neighbours())
    net = Net(ssem, rsem)
    srcs, fulls = (w_qkv, w_out, w_fc, w_proj), (f_qkv, f_out, f_fc, f_proj)
    gathers = [Gather(net, t, n, s, f, i % 2) for i, (n, s, f) in enumerate(zip(NAMES, srcs, fulls))]
    smalls = [net.send(small, f_small.at[t.x], t.at("x", s)) for s in (1, 3, 2)]
    local = []
    for k, (s, f) in enumerate(zip(srcs + (small,), fulls + (f_small,))):
        local.append(pltpu.make_async_copy(s, held[k], lsem.at[k]))
        local[-1].start()
    for n, step in enumerate(gather_steps(gathers)):
        step()
        if n == 4:
            for k, f in enumerate(fulls + (f_small,)):
                local[k].wait()
                local[k] = pltpu.make_async_copy(held[k], f.at[t.x], lsem.at[k])
                local[k].start()
    for g in gathers:
        g.finish()
    for copy in smalls:
        copy.wait_recv()
    for copy in local:
        copy.wait()
    net.finish()


def gather_weights(w_qkv, w_out, w_fc, w_proj, small):
    any_space = pl.BlockSpec(memory_space=pl.ANY)
    n = 320
    srcs = (w_qkv, w_out, w_fc, w_proj, small)
    return pl.pallas_call(
        gather_kernel,
        name="gather_weights",
        out_shape=[jax.ShapeDtypeStruct((4,) + s.shape, s.dtype) for s in srcs],
        in_specs=[any_space] * 5,
        out_specs=[any_space] * 5,
        scratch_shapes=[pltpu.SemaphoreType.DMA((n,)), pltpu.SemaphoreType.DMA((n,)), pltpu.SemaphoreType.DMA((5,))]
        + [pltpu.VMEM(s.shape, s.dtype) for s in srcs],
        compiler_params=pltpu.CompilerParams(collective_id=0, has_side_effects=True),
    )(*srcs)


N_SEM_A = 64


def dot_t(a, b):
    return lax.dot_general(a, b, (((1,), (1,)), ((), ())), preferred_element_type=F32)


def causal(s, i):
    rows = lax.broadcasted_iota(jnp.int32, (256, 256), 0)
    cols = lax.broadcasted_iota(jnp.int32, (256, 256), 1)
    last = jnp.where(cols <= rows, s[:, 256 * i :], -1e30)
    return last if i == 0 else jnp.concatenate([s[:, : 256 * i], last], axis=1)


class Swap:
    def __init__(self, net, torus, parts):
        self.net, self.t, self.parts = net, torus, parts

    def pack_single(self, full, single):
        parts = self.parts
        for d in range(4):
            cols = [full[:, 1280 * k + 1024 + 64 * d : 1280 * k + 1088 + 64 * d] for k in range(parts)]
            if parts % 2:
                cols.append(jnp.zeros((256, 64), BF16))
            single[d] = jnp.concatenate(cols, axis=1)

    def out_pairs(self, full, box):
        t, net, got = self.t, self.net, []
        for p in range(2):
            sent = []
            for s in (1, 3, 2):
                d = wrap(t.x + s)
                for k in range(self.parts):
                    cols = pl.ds(pl.multiple_of(1280 * k + 256 * d + 128 * p, 128), 128)
                    sent.append(net.send(full.at[:, cols], box.at[p, k, t.x], t.at("x", s)))
            got.append(sent)
        return got

    def keep_pairs(self, full, box):
        for p in range(2):
            for k in range(self.parts):
                cols = pl.ds(pl.multiple_of(1280 * k + 256 * self.t.x + 128 * p, 128), 128)
                box[p, k, self.t.x] = full[:, cols]

    def out_single(self, single, box):
        t = self.t
        sent = [self.net.send(single.at[wrap(t.x + s)], box.at[t.x], t.at("x", s)) for s in (1, 3, 2)]
        return sent

    def back_pair(self, p, src, full):
        t, net, sent = self.t, self.net, []
        for s in (1, 3, 2):
            d = wrap(t.x + s)
            for k in range(self.parts):
                cols = pl.ds(pl.multiple_of(1280 * k + 256 * t.x + 128 * p, 128), 128)
                sent.append(net.send(src.at[d, k, p], full.at[:, cols], t.at("x", s)))
        return sent

    def keep_back(self, p, src, full):
        for k in range(self.parts):
            cols = pl.ds(pl.multiple_of(1280 * k + 256 * self.t.x + 128 * p, 128), 128)
            full[:, cols] = src[self.t.x, k, p]

    def unpack_single(self, box, full):
        for k in range(self.parts):
            cols = [box[d, :, 64 * k : 64 * k + 64] for d in range(4)]
            full[:, 1280 * k + 1024 : 1280 * (k + 1)] = jnp.concatenate(cols, axis=1)


def wait_all(copies):
    for copy in copies:
        copy.wait_recv()


def fwd_kernel(qkv, att, heads, lse, box, single, single_in, res, res_single, res_single_in, full, outs, ssem, rsem):
    t = Torus()
    greet(t.neighbours("x", core=False))
    net = Net(ssem, rsem)
    swap = Swap(net, t, 3)
    got = swap.out_pairs(qkv, box)
    swap.pack_single(qkv, single)
    got_single = swap.out_single(single, single_in)
    swap.keep_pairs(qkv, box)
    single_in[t.x] = single[t.x]
    lse[...] = jnp.zeros_like(lse)
    back = Swap(net, t, 1)
    sent = []

    def take_pair(p):
        wait_all(got[p])
        for k in range(3):
            for s in range(4):
                for j in range(2):
                    v = box[p, k, s, :, 64 * j : 64 * j + 64]
                    heads[k, 2 * p + j, 256 * s : 256 * (s + 1), :] = v * BF16(0.125) if k == 0 else v

    def take_single():
        wait_all(got_single)
        for k in range(3):
            for s in range(4):
                v = single_in[s, :, 64 * k : 64 * k + 64]
                heads[k, 4, 256 * s : 256 * (s + 1), :] = v * BF16(0.125) if k == 0 else v

    def one_head(h, j):
        lane = lax.broadcasted_iota(jnp.int32, (256, 128), 1)
        for i in range(4):
            rows = slice(256 * i, 256 * (i + 1))
            n = 256 * (i + 1)
            s = causal(dot_t(heads[0, h, rows, :], heads[1, h, :n, :]), i)
            top = jnp.max(s, axis=1, keepdims=True)
            p = jnp.exp(s - top)
            total = jnp.sum(p, axis=1, keepdims=True)
            lse[rows, :] = jnp.where(lane == h, top + jnp.log(total), lse[rows, :])
            o = jnp.dot(p.astype(BF16), heads[2, h, :n, :], preferred_element_type=F32)
            outs[j, rows, :] = (o / total).astype(BF16)

    for p in range(2):
        take_pair(p)

        def body(j, _):
            one_head(2 * p + j, j)
            return 0

        lax.fori_loop(0, 2, body, 0)
        for i in range(4):
            rows = slice(256 * i, 256 * (i + 1))
            res[i, 0, p] = jnp.concatenate([outs[0, rows, :], outs[1, rows, :]], axis=1)
        sent += back.back_pair(p, res, full)
        back.keep_back(p, res, full)
    take_single()
    one_head(4, 0)
    for i in range(4):
        res_single[i] = jnp.concatenate([outs[0, 256 * i : 256 * (i + 1), :], jnp.zeros((256, 64), BF16)], axis=1)
    sent_single = back.out_single(res_single, res_single_in)
    res_single_in[t.x] = res_single[t.x]
    wait_all(sent_single)
    back.unpack_single(res_single_in, full)
    wait_all(sent)
    att[...] = full[...]
    net.finish()


def attention(qkv):
    vm = pl.BlockSpec(memory_space=pltpu.VMEM)
    return pl.pallas_call(
        fwd_kernel,
        name="attention",
        out_shape=[
            jax.ShapeDtypeStruct((256, 1280), BF16),
            jax.ShapeDtypeStruct((3, 5, 1024, 64), BF16),
            jax.ShapeDtypeStruct((1024, 128), F32),
        ],
        in_specs=[vm],
        out_specs=[vm] * 3,
        scratch_shapes=[
            pltpu.VMEM((2, 3, 4, 256, 128), BF16),
            pltpu.VMEM((4, 256, 256), BF16),
            pltpu.VMEM((4, 256, 256), BF16),
            pltpu.VMEM((4, 1, 2, 256, 128), BF16),
            pltpu.VMEM((4, 256, 128), BF16),
            pltpu.VMEM((4, 256, 128), BF16),
            pltpu.VMEM((256, 1280), BF16),
            pltpu.VMEM((2, 1024, 64), BF16),
            pltpu.SemaphoreType.DMA((N_SEM_A,)),
            pltpu.SemaphoreType.DMA((N_SEM_A,)),
        ],
        compiler_params=pltpu.CompilerParams(collective_id=3, has_side_effects=True, vmem_limit_bytes=48 << 20),
    )(qkv)


def bwd_kernel(datt, heads, lse, gqkv, box, single, single_in, do, res, res_single, res_single_in, full, dkv, grads, ssem, rsem):
    t = Torus()
    greet(t.neighbours("x", core=False))
    net = Net(ssem, rsem)
    swap = Swap(net, t, 1)
    got = swap.out_pairs(datt, box)
    swap.pack_single(datt, single)
    got_single = swap.out_single(single, single_in)
    swap.keep_pairs(datt, box)
    single_in[t.x] = single[t.x]
    back = Swap(net, t, 3)
    sent = []

    def one_head(h, j):
        lane = lax.broadcasted_iota(jnp.int32, (256, 128), 1)
        dkv[...] = jnp.zeros_like(dkv)
        for i in range(4):
            rows = slice(256 * i, 256 * (i + 1))
            n = 256 * (i + 1)
            q, k, v, d = heads[0, h, rows, :], heads[1, h, :n, :], heads[2, h, :n, :], do[h, rows, :]
            total = jnp.sum(jnp.where(lane == h, lse[rows, :], 0.0), axis=1, keepdims=True)
            p = jnp.exp(causal(dot_t(q, k), i) - total)
            t1 = p * dot_t(d, v)
            inner = jnp.sum(t1, axis=1, keepdims=True)
            ds = (t1 - p * inner).astype(BF16)
            grads[0, j, rows, :] = (jnp.dot(ds, k, preferred_element_type=F32) * 0.125).astype(BF16)
            dkv[0, :, :n] += jnp.dot(q.T, ds, preferred_element_type=F32)
            dkv[1, :, :n] += jnp.dot(d.T, p.astype(BF16), preferred_element_type=F32)
        for k in range(2):
            grads[1 + k, j] = dkv[k].T.astype(BF16)

    for p in range(2):
        wait_all(got[p])
        for s in range(4):
            for j in range(2):
                do[2 * p + j, 256 * s : 256 * (s + 1), :] = box[p, 0, s, :, 64 * j : 64 * j + 64]

        def body(j, _):
            one_head(2 * p + j, j)
            return 0

        lax.fori_loop(0, 2, body, 0)
        for i in range(4):
            rows = slice(256 * i, 256 * (i + 1))
            for k in range(3):
                res[i, k, p] = jnp.concatenate([grads[k, 0, rows, :], grads[k, 1, rows, :]], axis=1)
        sent += back.back_pair(p, res, full)
        back.keep_back(p, res, full)
    wait_all(got_single)
    for s in range(4):
        do[4, 256 * s : 256 * (s + 1), :] = single_in[s, :, :64]
    one_head(4, 0)
    for i in range(4):
        rows = slice(256 * i, 256 * (i + 1))
        cols = [grads[k, 0, rows, :] for k in range(3)] + [jnp.zeros((256, 64), BF16)]
        res_single[i] = jnp.concatenate(cols, axis=1)
    sent_single = back.out_single(res_single, res_single_in)
    res_single_in[t.x] = res_single[t.x]
    wait_all(sent_single)
    back.unpack_single(res_single_in, full)
    wait_all(sent)
    gqkv[...] = full[...]
    net.finish()


def attention_back(datt, heads, lse):
    vm = pl.BlockSpec(memory_space=pltpu.VMEM)
    return pl.pallas_call(
        bwd_kernel,
        name="attention_back",
        out_shape=jax.ShapeDtypeStruct((256, 3840), BF16),
        in_specs=[vm] * 3,
        out_specs=vm,
        scratch_shapes=[
            pltpu.VMEM((2, 1, 4, 256, 128), BF16),
            pltpu.VMEM((4, 256, 128), BF16),
            pltpu.VMEM((4, 256, 128), BF16),
            pltpu.VMEM((5, 1024, 64), BF16),
            pltpu.VMEM((4, 3, 2, 256, 128), BF16),
            pltpu.VMEM((4, 256, 256), BF16),
            pltpu.VMEM((4, 256, 256), BF16),
            pltpu.VMEM((256, 3840), BF16),
            pltpu.VMEM((2, 64, 1024), F32),
            pltpu.VMEM((3, 2, 1024, 64), BF16),
            pltpu.SemaphoreType.DMA((N_SEM_A,)),
            pltpu.SemaphoreType.DMA((N_SEM_A,)),
        ],
        compiler_params=pltpu.CompilerParams(collective_id=4, has_side_effects=True, vmem_limit_bytes=48 << 20),
    )(datt, heads, lse)


ORDERS = ("xyz", "yzx", "zxy")


def view(ref, chosen, rows):
    return ref.at[tuple(chosen.get(a, slice(None)) for a in "xyz") + (pl.ds(*rows),)]


def leading(ref):
    return ref.shape[:-2]


def add_into(dst, *srcs):
    lead = leading(dst)
    count = 1
    for n in lead:
        count *= n

    def slab(i):
        index = []
        for n in reversed(lead):
            index.append(lax.rem(i, n))
            i = i // n
        return tuple(reversed(index))

    def body(i, _):
        at = slab(i)
        total = dst[at].astype(F32)
        for s in srcs:
            total = total + s[at].astype(F32)
        dst[at] = total.astype(BF16)
        return 0

    if count == 1 and not lead:
        total = dst[...].astype(F32)
        for s in srcs:
            total = total + s[...].astype(F32)
        dst[...] = total.astype(BF16)
    else:
        lax.fori_loop(0, count, body, 0)


def inbox_shapes(classes):
    out = []
    for (order, _, n) in classes:
        half = [2 if a == order[1] else 4 for a in "xyz" if a != order[0]]
        whole = [4, 4]
        out += [half + [n, 128]] * 2 + [whole + [n, 128]] * 2
        out += [[2, n, 128]] * 2 + [[4, n, 128]] * 2
        out += [[3, n, 128]]
    return [pltpu.VMEM(tuple(s), BF16) for s in out]


PER_CLASS = 9


class Lane:
    def __init__(self, net, torus, acc, inbox, order, row, n):
        self.net, self.t, self.acc, self.inbox, self.order = net, torus, acc, inbox, order
        self.rows = (row, n)
        self.fixed = {}
        self.got = {}

    def halves(self, phase):
        a = self.order[phase + 1]
        return [{a: pl.ds(0, 2)}, {a: pl.ds(2, 2)}]

    def box_half(self, box, phase, half):
        if phase == 1:
            return box.at[pl.ds(2 * half, 2)]
        left = [a for a in "xyz" if a != self.order[0]]
        cut = left.index(self.order[1])
        return box.at[(slice(None),) * cut + (pl.ds(2 * half, 2),)]

    def first(self, phase):
        axis = self.order[phase]
        p = self.t.pos(axis)
        h = self.halves(phase)
        b = self.inbox[4 * phase : 4 * phase + 4]
        at = lambda shift, cut: view(self.acc, {**self.fixed, axis: wrap(p + shift), **cut}, self.rows)
        up, down = self.t.at(axis, 1), self.t.at(axis, 3)
        far = [self.net.send(at(2, h[0]), b[0], up), self.net.send(at(2, h[1]), b[1], down)]
        near = [
            self.net.send(at(1, h[1]), self.box_half(b[2], phase, 1), up),
            self.net.send(at(3, h[0]), self.box_half(b[3], phase, 0), down),
        ]
        self.got[phase] = (far, near)

    def second(self, phase):
        axis = self.order[phase]
        p = self.t.pos(axis)
        h = self.halves(phase)
        b = self.inbox[4 * phase : 4 * phase + 4]
        at = lambda shift, cut: view(self.acc, {**self.fixed, axis: wrap(p + shift), **cut}, self.rows)
        up, down = self.t.at(axis, 1), self.t.at(axis, 3)
        far, near = self.got[phase]
        far[0].wait_recv()
        add_into(at(1, h[0]), b[0])
        near.append(self.net.send(at(1, h[0]), self.box_half(b[2], phase, 0), up))
        far[1].wait_recv()
        add_into(at(3, h[1]), b[1])
        near.append(self.net.send(at(3, h[1]), self.box_half(b[3], phase, 1), down))

    def third(self, phase):
        axis = self.order[phase]
        p = self.t.pos(axis)
        b = self.inbox[4 * phase : 4 * phase + 4]
        for copy in self.got[phase][1]:
            copy.wait_recv()
        self.fixed[axis] = p
        add_into(view(self.acc, self.fixed, self.rows), b[2], b[3])

    def last(self):
        axis = self.order[2]
        p = self.t.pos(axis)
        box = self.inbox[8]
        self.got[2] = [
            self.net.send(view(self.acc, {**self.fixed, axis: wrap(p + s)}, self.rows), box.at[s - 1], self.t.at(axis, s))
            for s in (1, 3, 2)
        ]

    def done(self):
        axis = self.order[2]
        for copy in self.got[2]:
            copy.wait_recv()
        self.fixed[axis] = self.t.pos(axis)
        box = self.inbox[8]
        add_into(view(self.acc, self.fixed, self.rows), box.at[0], box.at[1], box.at[2])


class Spread:
    def __init__(self, net, torus, acc, out, order, row, n, sem):
        self.net, self.t, self.out, self.order, self.rows, self.sem = net, torus, out, order, (row, n), sem
        self.own = view(acc, {"x": torus.x, "y": torus.y, "z": torus.z}, self.rows)

    def place(self, y, z):
        return self.out.at[self.t.c, y, z, pl.ds(*self.rows)]

    def band(self, v, b=slice(None)):
        y, z = (b, v) if self.order == "yz" else (v, b)
        return self.place(y, z)

    def start(self):
        t = self.t
        here = self.place(t.y, t.z)
        self.keep = pltpu.make_async_copy(self.own, here, self.sem)
        self.keep.start()
        self.first = [self.net.send(self.own, here, t.at(self.order[0], s)) for s in (1, 3, 2)]

    def second(self):
        t, axis = self.t, self.order[1]
        for copy in self.first:
            copy.wait_recv()
        self.keep.wait()
        here = self.band(t.pos(axis))
        self.near = [self.net.send(here, here, t.at(axis, s)) for s in (1, 3)]

    def third(self):
        t, axis = self.t, self.order[1]
        p = t.pos(axis)
        self.far = []
        for copy, shift, to, b in ((self.near[0], 3, 1, pl.ds(0, 2)), (self.near[1], 1, 3, pl.ds(2, 2))):
            copy.wait_recv()
            there = self.band(wrap(p + shift), b)
            self.far.append(self.net.send(there, there, t.at(axis, to)))

    def share(self):
        for copy in self.far:
            copy.wait_recv()
        whole = self.place(slice(None), slice(None))
        self.core = self.net.send(whole, whole, self.t.sibling())

    def finish(self):
        self.core.wait_recv()


def reduce_steps(lanes, spreads):
    steps = []
    for phase in (0, 1):
        for what in ("first", "second", "third"):
            if phase == 0 and what == "first":
                continue
            for lane in lanes:
                steps.append((lambda lane=lane, what=what, phase=phase: getattr(lane, what)(phase)))
    for what in ("last", "done"):
        for lane in lanes:
            steps.append(getattr(lane, what))
            if what == "done":
                steps += [s.start for owner, s in spreads if owner is lane]
    for what in ("second", "third", "share", "finish"):
        steps += [getattr(s, what) for _, s in spreads]
    return steps


def store_blocks(acc, x, first, unit, blocks, rows):
    at = 0
    for block in blocks:
        done = 0
        while done < 320:
            n = min(320 - done, rows - at % rows)
            s = at // rows
            slab = first + s
            acc[x, slab // 4, lax.rem(slab, 4), pl.ds(at % rows, n), :] = block[done : done + n]
            done += n
            at += n


GROUPS = {
    "mlp": (800, (272, 272, 272)),
    "attn": (400, (144, 144, 128)),
}


def classes_of(group):
    row, out = 0, []
    for order, n in zip(ORDERS, GROUPS[group][1]):
        out.append((order, row, n))
        row += n
    return out


def spreads_of(group):
    a, b, c = classes_of(group)
    h = c[2] // 32 * 16
    return [(0, "yz", a[1], a[2]), (1, "zy", b[1], b[2]), (2, "yz", c[1], h), (2, "zy", c[1] + h, c[2] - h)]


def scratch_of(group):
    rows = GROUPS[group][0] + 16
    return [pltpu.VMEM((4, 4, 4, rows, 128), BF16)] + inbox_shapes(classes_of(group))


def begin_reduce(group, net, torus, acc, inbox, out, sems):
    lanes = [
        Lane(net, torus, acc, inbox[PER_CLASS * k : PER_CLASS * (k + 1)], *c) for k, c in enumerate(classes_of(group))
    ]
    spreads = [
        (lanes[k], Spread(net, torus, acc, out, order, row, n, sems.at[i]))
        for i, (k, order, row, n) in enumerate(spreads_of(group))
    ]
    return lanes, spreads


def store_small(acc, total, rows):
    for x in range(4):
        for y in range(4):
            for z in range(4):
                k = y * 4 + z
                v = total[x, 16 * k : 16 * k + 16, :] if k < 2 else jnp.zeros((16, 128), F32)
                acc[x, y, z, pl.ds(rows, 16), :] = v.astype(BF16)


def product(lhs, rhs, acc, x, first, unit, rows):
    out = jnp.dot(lhs, rhs, preferred_element_type=F32).astype(BF16)
    store_blocks(acc, x, first, unit, [out[:, 128 * t : 128 * (t + 1)] for t in range(5)], rows)


N_SEM = 100


def mlp_kernel(n2t, actt, gp, cot, small, out, n2t_v, actt_v, gp_v, cot_v, small_v, ssem, rsem, lsem, acc, *inbox):
    t = Torus()
    greet(t.neighbours())
    net = Net(ssem, rsem)
    sib, c = t.sibling(), t.c
    copies, local = [], []

    def both(src, own_dst, other_dst, own_src=None):
        copies.append(net.send(src, other_dst, sib))
        k = len(local)
        local.append(pltpu.make_async_copy(src if own_src is None else own_src, own_dst, lsem.at[k]))
        local[-1].start()

    both(n2t, n2t_v.at[:, pl.ds(0, 256)], n2t_v.at[:, pl.ds(256, 256)])
    both(cot, cot_v.at[pl.ds(0, 256)], cot_v.at[pl.ds(256, 256)])
    for s in range(4):
        mine, theirs = s * 1280 + c * 640, s * 1280 + (1 - c) * 640
        both(
            gp.at[:, pl.ds(pl.multiple_of(theirs, 128), 640)],
            gp_v.at[s, pl.ds(0, 256)], gp_v.at[s, pl.ds(256, 256)],
            gp.at[:, pl.ds(pl.multiple_of(mine, 128), 640)],
        )
        both(
            actt.at[pl.ds(pl.multiple_of(theirs, 16), 640)],
            actt_v.at[pl.ds(s * 640, 640), pl.ds(0, 256)], actt_v.at[pl.ds(s * 640, 640), pl.ds(256, 256)],
            actt.at[pl.ds(pl.multiple_of(mine, 16), 640)],
        )
    both(small, small_v.at[0], small_v.at[1])
    for copy in copies:
        copy.wait_recv()
    for copy in local:
        copy.wait()
    small_v[0] = small_v[0] + small_v[1]
    store_small(acc, small_v.at[0], 800)

    def fc(i, _):
        x, s = i // 4, lax.rem(i, 4)
        product(n2t_v[pl.ds(pl.multiple_of(x * 320, 16), 320), :], gp_v[s], acc, x, s * 2, 2, 800)
        return 0

    lax.fori_loop(0, 16, fc, 0)

    def proj(i, _):
        x, sub = i // 2, lax.rem(i, 2)
        lhs = actt_v[pl.ds(pl.multiple_of(i * 320, 16), 320), :]
        for half in range(2):
            product(lhs, cot_v[:, 640 * half : 640 * (half + 1)], acc, x, 8 + sub * 4 + half * 2, 2, 800)
        return 0

    lax.fori_loop(0, 8, proj, 0)
    lanes, spreads = begin_reduce("mlp", net, t, acc, inbox, out, lsem)
    for lane in lanes:
        lane.first(0)
    for step in reduce_steps(lanes, spreads):
        step()
    net.finish()


def reduce_mlp(n2t, actt, gp, cot, small):
    anys = pl.BlockSpec(memory_space=pl.ANY)
    return pl.pallas_call(
        mlp_kernel,
        name="reduce_mlp",
        out_shape=jax.ShapeDtypeStruct((2, 4, 4, 816, 128), BF16),
        in_specs=[anys] * 5,
        out_specs=anys,
        scratch_shapes=[
            pltpu.VMEM((1280, 512), BF16),
            pltpu.VMEM((2560, 512), BF16),
            pltpu.VMEM((4, 512, 640), BF16),
            pltpu.VMEM((512, 1280), BF16),
            pltpu.VMEM((2, 4, 32, 128), F32),
            pltpu.SemaphoreType.DMA((N_SEM,)),
            pltpu.SemaphoreType.DMA((N_SEM,)),
            pltpu.SemaphoreType.DMA((16,)),
        ]
        + scratch_of("mlp"),
        compiler_params=pltpu.CompilerParams(collective_id=1, has_side_effects=True, vmem_limit_bytes=56 << 20),
    )(n2t, actt, gp, cot, small)


def attn_kernel(n1t, gqkv, attt, gb, small, out, n1t_v, gqkv_v, attt_v, gb_v, small_v, ssem, rsem, lsem, acc, *inbox):
    t = Torus()
    greet(t.neighbours())
    net = Net(ssem, rsem)
    sib, c = t.sibling(), t.c
    copies, local = [], []

    def both(src, own_dst, other_dst, own_src=None):
        copies.append(net.send(src, other_dst, sib))
        k = len(local)
        local.append(pltpu.make_async_copy(src if own_src is None else own_src, own_dst, lsem.at[k]))
        local[-1].start()

    both(n1t, n1t_v.at[:, pl.ds(0, 256)], n1t_v.at[:, pl.ds(256, 256)])
    both(attt, attt_v.at[:, pl.ds(0, 256)], attt_v.at[:, pl.ds(256, 256)])
    for s in range(3):
        mine, theirs = c * 1920 + s * 640, (1 - c) * 1920 + s * 640
        both(
            gqkv.at[:, pl.ds(pl.multiple_of(theirs, 128), 640)],
            gqkv_v.at[s, pl.ds(0, 256)], gqkv_v.at[s, pl.ds(256, 256)],
            gqkv.at[:, pl.ds(pl.multiple_of(mine, 128), 640)],
        )
    both(
        gb.at[:, pl.ds(pl.multiple_of((1 - c) * 640, 128), 640)], gb_v.at[pl.ds(0, 256)], gb_v.at[pl.ds(256, 256)],
        gb.at[:, pl.ds(pl.multiple_of(c * 640, 128), 640)],
    )
    both(small, small_v.at[0], small_v.at[1])
    for copy in copies:
        copy.wait_recv()
    for copy in local:
        copy.wait()
    small_v[0] = small_v[0] + small_v[1]
    store_small(acc, small_v.at[0], 400)

    def qkv(i, _):
        x, s = i // 3, lax.rem(i, 3)
        product(n1t_v[pl.ds(pl.multiple_of(x * 320, 16), 320), :], gqkv_v[s], acc, x, s * 4, 4, 400)
        return 0

    lax.fori_loop(0, 12, qkv, 0)

    def outp(x, _):
        product(attt_v[pl.ds(pl.multiple_of(x * 320, 16), 320), :], gb_v[...], acc, x, 12, 4, 400)
        return 0

    lax.fori_loop(0, 4, outp, 0)
    lanes, spreads = begin_reduce("attn", net, t, acc, inbox, out, lsem)
    for lane in lanes:
        lane.first(0)
    for step in reduce_steps(lanes, spreads):
        step()
    net.finish()


def reduce_attn(n1t, gqkv, attt, gb, small):
    anys = pl.BlockSpec(memory_space=pl.ANY)
    return pl.pallas_call(
        attn_kernel,
        name="reduce_attn",
        out_shape=jax.ShapeDtypeStruct((2, 4, 4, 416, 128), BF16),
        in_specs=[anys] * 5,
        out_specs=anys,
        scratch_shapes=[
            pltpu.VMEM((1280, 512), BF16),
            pltpu.VMEM((3, 512, 640), BF16),
            pltpu.VMEM((1280, 512), BF16),
            pltpu.VMEM((512, 640), BF16),
            pltpu.VMEM((2, 4, 32, 128), F32),
            pltpu.SemaphoreType.DMA((N_SEM,)),
            pltpu.SemaphoreType.DMA((N_SEM,)),
            pltpu.SemaphoreType.DMA((16,)),
        ]
        + scratch_of("attn"),
        compiler_params=pltpu.CompilerParams(collective_id=2, has_side_effects=True, vmem_limit_bytes=56 << 20),
    )(n1t, gqkv, attt, gb, small)


def unpack_mlp_kernel(src, fc, proj):
    q = pl.program_id(1)
    flat = [src[0, 0, i, :800].astype(F32) for i in range(2)]
    flat = jnp.concatenate(flat, axis=0)

    @pl.when(q < 4)
    def _():
        for k in range(5):
            fc[:, 128 * k : 128 * (k + 1)] = flat[320 * k : 320 * (k + 1)]

    @pl.when(q >= 4)
    def _():
        for k in range(5):
            proj[:, 128 * k : 128 * (k + 1)] = flat[320 * k : 320 * (k + 1)]


def unpack_mlp(packed):
    return pl.pallas_call(
        unpack_mlp_kernel,
        name="unpack_mlp",
        grid=(2, 8),
        out_shape=[jax.ShapeDtypeStruct((320, 5120), F32), jax.ShapeDtypeStruct((1280, 1280), F32)],
        in_specs=[pl.BlockSpec((1, 1, 2, 816, 128), lambda c, q: (c, q // 2, q % 2, 0, 0))],
        out_specs=[
            pl.BlockSpec((320, 640), lambda c, q: (0, jnp.where(q < 4, q * 2 + c, 6 + c))),
            pl.BlockSpec((320, 640), lambda c, q: (c * 2 + jnp.where(q < 4, 0, (q - 4) // 2), jnp.where(q < 4, 0, q % 2))),
        ],
    )(packed)


def unpack_attn_kernel(src, qkv, out):
    q = pl.program_id(1)
    flat = jnp.concatenate([src[0, 0, i, :400].astype(F32) for i in range(4)], axis=0)

    @pl.when(q < 3)
    def _():
        for k in range(5):
            qkv[:, 128 * k : 128 * (k + 1)] = flat[320 * k : 320 * (k + 1)]

    @pl.when(q == 3)
    def _():
        for k in range(5):
            out[:, 128 * k : 128 * (k + 1)] = flat[320 * k : 320 * (k + 1)]


def unpack_attn(packed):
    return pl.pallas_call(
        unpack_attn_kernel,
        name="unpack_attn",
        grid=(2, 4),
        out_shape=[jax.ShapeDtypeStruct((320, 3840), F32), jax.ShapeDtypeStruct((320, 1280), F32)],
        in_specs=[pl.BlockSpec((1, 1, 4, 416, 128), lambda c, q: (c, q, 0, 0, 0))],
        out_specs=[
            pl.BlockSpec((320, 640), lambda c, q: (0, c * 3 + jnp.minimum(q, 2))),
            pl.BlockSpec((320, 640), lambda c, q: (0, c)),
        ],
    )(packed)


def unpack_small(packed, rows, count):
    return packed[0, 0, 0:2, rows:, :].astype(F32).reshape(-1)[:count]


HEAD_DIM = 64
EPS = 1e-05
GELU_A, GELU_B = 0.7978845608028654, 0.044715


def norm(v):
    center = v - jnp.mean(v, axis=-1, keepdims=True)
    scale = lax.rsqrt(jnp.mean(center * center, axis=-1, keepdims=True) + EPS)
    return center * scale, scale


def norm_back(grad, hat, scale, gain):
    inner = grad * gain
    rows = scale * (
        inner - jnp.mean(inner, axis=-1, keepdims=True) - hat * jnp.mean(inner * hat, axis=-1, keepdims=True)
    )
    return rows, jnp.sum(grad * hat, axis=0), jnp.sum(grad, axis=0)


def dot(a, b):
    return jnp.dot(a, b, preferred_element_type=F32)


def dot_cols(a, b):
    return lax.dot_general(a, b, (((1,), (1,)), ((), ())), preferred_element_type=F32)


def small_rows(*vectors):
    flat = jnp.concatenate([v.reshape(4, -1) for v in vectors], axis=1)
    return jnp.pad(flat, ((0, 0), (0, 4096 - flat.shape[1]))).reshape(4, 32, 128)


def shards(
    tokens,
    cotangent,
    ln1_gain,
    ln1_bias,
    w_qkv,
    qv_bias,
    w_out,
    out_bias,
    ln2_gain,
    ln2_bias,
    w_fc,
    fc_bias,
    w_proj,
    proj_bias,
):
    own = (ln1_gain, ln1_bias, qv_bias, out_bias, ln2_gain, ln2_bias, fc_bias, proj_bias)
    small = jnp.concatenate(own + (jnp.zeros((256,), BF16),)).reshape(32, 128)
    f_qkv, f_out, f_fc, f_proj, f_small = gather_weights(w_qkv, w_out, w_fc, w_proj, small)
    f_qkv, f_out, f_fc, f_proj = (
        f_qkv.reshape(1280, 3840),
        f_out.reshape(1280, 1280),
        f_fc.reshape(1280, 5120),
        f_proj.reshape(5120, 1280),
    )
    f_small = f_small.reshape(4, 4096).astype(F32)
    params, at = [], 0
    for v in own:
        params.append(f_small[:, at : at + v.shape[0]].reshape(-1))
        at += v.shape[0]
    gain_one, shift_one, bias_qv, bias_out, gain_two, shift_two, bias_fc, bias_proj = params

    rows = tokens[0].astype(F32)
    hat_one, scale_one = norm(rows)
    normed_one = (hat_one * gain_one + shift_one).astype(BF16)
    bias_qkv = jnp.concatenate([bias_qv[:1280], jnp.zeros((1280,), F32), bias_qv[1280:]])
    qkv = (dot(normed_one, f_qkv) + bias_qkv).astype(BF16)
    attended, heads, lse = attention(qkv)
    middle = rows + dot(attended, f_out) + bias_out
    hat_two, scale_two = norm(middle)
    normed_two = (hat_two * gain_two + shift_two).astype(BF16)
    pre = dot(normed_two, f_fc) + bias_fc
    bend = jnp.tanh(GELU_A * (pre + GELU_B * pre * pre * pre))
    act = (0.5 * pre * (1.0 + bend)).astype(BF16)
    block_out = (middle + dot(act, f_proj) + bias_proj).astype(BF16)

    cot = cotangent[0]
    cot_rows = cot.astype(F32)
    slope = 0.5 * (1.0 + bend) + 0.5 * pre * (1.0 - bend * bend) * GELU_A * (1.0 + 3.0 * GELU_B * pre * pre)
    grad_pre = (dot_cols(cot, f_proj) * slope).astype(BF16)
    grad_two, grad_gain_two, grad_shift_two = norm_back(dot_cols(grad_pre, f_fc), hat_two, scale_two, gain_two)
    grad_middle = cot_rows + grad_two
    grad_branch = grad_middle.astype(BF16)
    small_mlp = small_rows(
        grad_gain_two, grad_shift_two, jnp.sum(grad_pre.astype(F32), axis=0), jnp.sum(cot_rows, axis=0)
    )
    packed_mlp = reduce_mlp(normed_two.T, act.T, grad_pre, cot, small_mlp)

    grad_attended = dot_cols(grad_branch, f_out).astype(BF16)
    grad_qkv = attention_back(grad_attended, heads, lse)
    grad_one, grad_gain_one, grad_shift_one = norm_back(dot_cols(grad_qkv, f_qkv), hat_one, scale_one, gain_one)
    grad_tokens = (grad_middle + grad_one).astype(BF16)
    sums = jnp.sum(grad_qkv.astype(F32), axis=0)
    small_attn = small_rows(
        grad_gain_one,
        grad_shift_one,
        jnp.concatenate([sums[:1280], sums[2560:]]),
        jnp.sum(grad_branch.astype(F32), axis=0),
    )
    packed_attn = reduce_attn(normed_one.T, grad_qkv, attended.T, grad_branch, small_attn)

    g_fc, g_proj = unpack_mlp(packed_mlp)
    g_qkv, g_out = unpack_attn(packed_attn)
    s_mlp = unpack_small(packed_mlp, 800, 2240)
    s_attn = unpack_small(packed_attn, 400, 1600)
    return (
        block_out[None],
        grad_tokens[None],
        s_attn[:320],
        s_attn[320:640],
        g_qkv,
        s_attn[640:1280],
        g_out,
        s_attn[1280:1600],
        s_mlp[:320],
        s_mlp[320:640],
        g_fc,
        s_mlp[640:1920],
        g_proj,
        s_mlp[1920:2240],
    )


def solution(mesh):
    vector, matrix, batch = P("shard"), P("shard", None), P("rep", "shard", None)
    placed = (batch, batch, vector, vector, matrix, vector, matrix, vector, vector, vector, matrix, vector, matrix, vector)
    return jax.shard_map(shards, mesh=mesh, in_specs=placed, out_specs=placed, check_vma=False)
```

time: 1210 us -> 480 us (0.40)
  waiting for transfers between devices: 777 us -> 0 us
  Pallas kernels: 0 us -> 373 us
  blocking collectives: 183 us -> 0 us
  matrix products: 152 us -> 60.8 us
  other arithmetic: 47.3 us -> 12.6 us
  between operations: 17.5 us -> 1.1 us
    reduce_scatter x6 -> x0, waiting for transfers between devices: 409 us -> none  [the longest x1 121 us: shards(): lax.psum_scatter(grad_proj_w.astype(jnp.bfloat16), 'shard', scatter_dimen...]
    pallas_call x0 -> x7, Pallas kernels: none -> 373 us  [the longest x1 105 us: reduce_mlp(): pl.pallas_call(mlp_kernel, name='reduce_mlp', out_shape=jax.ShapeDtypeStr...]
    all_gather x6 -> x0, waiting for transfers between devices: 364 us -> none  [the longest x1 120 us: shards(): lax.all_gather(w_fc, 'shard', axis=0, tiled=True)]
    psum x1 -> x0, blocking collectives: 126 us -> none  [sum_attn(): lax.psum(grads[0].astype(jnp.bfloat16), 'rep').astype(jnp.float32)]
    dot_general x18 -> x8, matrix products: 152 us -> 60.8 us  [the longest x4 34.2 us: dot(): return jnp.dot(a, b, preferred_element_type=F32)]
    convert_element_type x21 -> x0, other arithmetic: 33 us -> none  [the longest x1 14.5 us: shards(): (prob_full * (grad_probs - inner_sum)).astype(jnp.bfloat16)]
    unnamed x2 -> x0, blocking collectives: 32.5 us -> none
    all_gather x2 -> x0, blocking collectives: 24.1 us -> none  [the longest x1 12.2 us: shards(): lax.all_gather(qv_bias, 'shard', axis=0, tiled=True)]
  transfers between devices with their start and end apart: 13 -> 0, of which waited for: 11 -> 0; matrix products, arithmetic and copies ran while one was open for 13% -> 0% of each run, Pallas kernels for 0% -> 0%
where the time goes in v1:
time: 480 us; the launch traced here: 471 us
  Pallas kernels  373 us (78%)
  matrix products  60.8 us (13%)
  local copies, waits for them, and re-layouts  23.2 us (5%)
  other arithmetic  12.6 us (3%)
    pallas_call x1, Pallas kernels, reduce_mlp(): pl.pallas_call(mlp_kernel, name='reduce_mlp', out_shape=jax.ShapeDtypeStr...  105 us
    pallas_call x1, Pallas kernels, gather_weights(): pl.pallas_call(gather_kernel, name='gather_weights', out_shape=[jax.Shape...  101 us
    pallas_call x1, Pallas kernels, reduce_attn(): pl.pallas_call(attn_kernel, name='reduce_attn', out_shape=jax.ShapeDtypeS...  69.4 us
    pallas_call x1, Pallas kernels, attention_back(): pl.pallas_call(bwd_kernel, name='attention_back', out_shape=jax.ShapeDtyp...  39.3 us
    pallas_call x1, Pallas kernels, attention(): pl.pallas_call(fwd_kernel, name='attention', out_shape=[jax.ShapeDtypeStr...  39.2 us
    dot_general x4, matrix products, dot(): return jnp.dot(a, b, preferred_element_type=F32)  34.2 us
    dot_general x4, matrix products, dot_cols(): lax.dot_general(a, b, (((1,), (1,)), ((), ())), preferred_element_type=F32)  26.6 us
    pallas_call x1, Pallas kernels, unpack_mlp(): pl.pallas_call(unpack_mlp_kernel, name='unpack_mlp', grid=(2, 8), out_sha...  12.9 us

profile of v1, /device:TPU:0, one launch (start us, length us, event | category | flops | bytes accessed | tf_op | source)
XLA Modules:
  0.0 470.9 jit_solution(17316821724199046171)
XLA Ops:
  0.6 1.3 convert_reduce_fusion.2
  1.9 1.4 fusion.36
  3.3 6.2 %concatenate.16 = bf16[4096]{0:T(1024)(128)(2,1)} concatenate(bf16[320]{0:T(512)(128)(2,1)} %param.16, bf16[320]{0:T(512)(128)(2,1)} %param.17, bf16[640]{0:T(1024)(128)(2,1)} %param.19, bf16[320]{0:T(512)(128)(2,1)} %param.21, bf16[320]{0:T(512)(128)(2,1)} %param.22, bf16[320]{0:T(512)(128)(2,1)} %param.23, bf16[1280]{0:T(1024)(128)(2,1)} %param.25, bf16[320]{0:T(512)(128)(2,1)} %param.27, ...), dimensions={0} | concatenate | bytes 16384 | tf_op jit(solution)/shard_map/concatenate | solution.py:1078
  9.5 100.5 %gather_weights.1 = (bf16[4,320,3840]{2,1,0:T(8,128)(2,1)}, bf16[4,320,1280]{2,1,0:T(8,128)(2,1)}, bf16[4,320,5120]{2,1,0:T(8,128)(2,1)}, bf16[4,1280,1280]{2,1,0:T(8,128)(2,1)}, bf16[4,32,128]{2,1,0:T(8,128)(2,1)}) custom-call(bf16[320,3840]{1,0:T(8,128)(2,1)} %w_qkv.1, bf16[320,1280]{1,0:T(8,128)(2,1)} %w_out.1, bf16[320,5120]{1,0:T(8,128)(2,1)} %w_fc.1, ...), custom_call_target="tpu_custom_call" | custom-call | tf_op jit(solution)/shard_map/gather_weights/pallas_call | solution.py:276
  110.1 0.8 convert_bitcast_fusion.1
  111.6 6.6 %fusion.12.qkv = bf16[256,3840]{1,0:T(8,128)(2,1)S(1)} fusion(bf16[1280,3840]{1,0:T(8,128)(2,1)} %bitcast.123, f32[3840]{0:T(1024)S(1)} %pad_maximum_fusion, bf16[1,256,1280]{2,1,0:T(8,128)(2,1)S(1)} %copy-done.1, f32[1280]{0:T(1024)S(1)} %add.119, f32[1280]{0:T(1024)S(1)} %mul.176, f32[256]{0:T(256)S(1)} %add_rsqrt_fusion.1, ...), kind=kOutput, calls=%fused_computation.21 | convolution fusion | flops 2520514560 | bytes 12479488 | tf_op jit(solution)/shard_map/dot_general | solution.py:1049
  118.2 39.2 %attention.1 = (bf16[256,1280]{1,0:T(8,128)(2,1)S(1)}, bf16[3,5,1024,64]{3,2,1,0:T(8,128)(2,1)}, f32[1024,128]{1,0:T(8,128)S(1)}) custom-call(bf16[256,3840]{1,0:T(8,128)(2,1)S(1)} %fusion.12.qkv), custom_call_target="tpu_custom_call" | custom-call | tf_op jit(solution)/shard_map/attention/pallas_call | solution.py:432
  157.4 1.1 copy.28
  158.5 3.0 fusion.60
  161.8 12.8 %fusion.11 = (bf16[5120,256]{0,1:T(8,128)(2,1)}, f32[256,5120]{1,0:T(8,128)}) fusion(f32[5120]{0:T(1024)S(1)} %add.132, bf16[1280,5120]{1,0:T(8,128)(2,1)} %bitcast.119, f32[256,1280]{1,0:T(8,128)S(1)} %get-tuple-element.69, f32[1280]{0:T(1024)S(1)} %add.129, f32[1280]{0:T(1024)S(1)} %mul.182, f32[256]{0:T(256)S(1)} %add_rsqrt_fusion, ...), kind=kOutput, calls=%fused_computation.17 | convolution fusion | flops 3370188800 | bytes 22315008 | tf_op jit(solution)/shard_map/dot_general | solution.py:1049
  174.7 4.8 %copy.31.actt = bf16[5120,256]{1,0:T(8,128)(2,1)} copy(bf16[5120,256]{0,1:T(8,128)(2,1)} %get-tuple-element.70) | data formatting | bytes 5242880 | tf_op jit(solution)/shard_map/convert_element_type | solution.py:1104
  179.5 11.8 %fusion.20 = bf16[1,256,1280]{2,1,0:T(8,128)(2,1)} fusion(f32[256,1280]{1,0:T(8,128)S(1)} %get-tuple-element.69, bf16[5120,1280]{1,0:T(8,128)(2,1)} %bitcast.121, f32[256,5120]{1,0:T(8,128)} %get-tuple-element.71, f32[1280]{0:T(1024)S(1)} %add.138), kind=kOutput, calls=%fused_computation.33 | convolution fusion | flops 3368222720 | bytes 20321280 | tf_op jit(solution)/shard_map/dot_general | solution.py:1049
  191.3 8.6 %convert_reduce_fusion = (f32[5120]{0:T(1024)S(1)}, bf16[256,5120]{1,0:T(8,128)(2,1)S(1)}) fusion(f32[256,5120]{1,0:T(8,128)S(1)} %copy-done.8, bf16[5120,1280]{1,0:T(8,128)(2,1)} %bitcast.122, bf16[1,256,1280]{2,1,0:T(8,128)(2,1)S(1)} %copy-done.4), kind=kOutput, calls=%fused_computation.19 | convolution fusion | flops 3382963200 | bytes 21647360 | tf_op jit(solution)/shard_map/dot_general | solution.py:1053
  199.9 8.6 %fusion.61 = f32[256,1280]{1,0:T(8,128)} fusion(bf16[256,5120]{1,0:T(8,128)(2,1)S(1)} %get-tuple-element.73.gp, bf16[1280,5120]{1,0:T(8,128)(2,1)} %bitcast.120), kind=kOutput, calls=%fused_computation.102 | convolution fusion | flops 3355443200 | bytes 17039360 | tf_op jit(solution)/shard_map/dot_general | solution.py:1053
  208.6 2.7 multiply_reduce_fusion
  211.3 3.2 convert_reduce_fusion.4
  214.5 1.0 convolution_convert_fusion.datt
  215.6 39.3 %attention_back.1.gqkv = bf16[256,3840]{1,0:T(8,128)(2,1)S(1)} custom-call(bf16[256,1280]{1,0:T(8,128)(2,1)S(1)} %convolution_convert_fusion.datt, bf16[3,5,1024,64]{3,2,1,0:T(8,128)(2,1)} %get-tuple-element.32.heads, f32[1024,128]{1,0:T(8,128)S(1)} %get-tuple-element.33.lse), custom_call_target="tpu_custom_call" | custom-call | tf_op jit(solution)/shard_map/attention_back/pallas_call | solution.py:525
  254.9 8.3 %fusion.62 = f32[256,1280]{1,0:T(8,128)} fusion(bf16[256,3840]{1,0:T(8,128)(2,1)S(1)} %attention_back.1.gqkv, bf16[1280,3840]{1,0:T(8,128)(2,1)} %bitcast.124), kind=kOutput, calls=%fused_computation.103 | convolution fusion | flops 2516582400 | bytes 13107200 | tf_op jit(solution)/shard_map/dot_general | solution.py:1053
  264.6 2.3 copy.30.n2t
  266.9 1.4 fusion.35
  268.3 1.3 fusion.44
  269.9 0.6 copy.39
  270.5 2.2 copy.29.n1t
  272.7 69.4 %reduce_attn.1.src = bf16[2,4,4,416,128]{4,3,2,1,0:T(8,128)(2,1)} custom-call(bf16[1280,256]{1,0:T(8,128)(2,1)} %copy.29.n1t, bf16[256,3840]{1,0:T(8,128)(2,1)} %copy-done, bf16[1280,256]{1,0:T(8,128)(2,1)} %bitcast.108, bf16[256,1280]{1,0:T(8,128)(2,1)} %copy-done.6, f32[4,32,128]{2,1,0:T(8,128)} %bitcast.113), custom_call_target="tpu_custom_call" | custom-call | tf_op jit(solution)/shard_map/reduce_attn/pallas_call | solution.py:945
  342.1 0.7 slice.117
  343.4 0.7 fusion.59
  344.1 104.7 %reduce_mlp.1.src = bf16[2,4,4,816,128]{4,3,2,1,0:T(8,128)(2,1)} custom-call(bf16[1280,256]{1,0:T(8,128)(2,1)} %copy.30.n2t, bf16[5120,256]{1,0:T(8,128)(2,1)} %copy.31.actt, bf16[256,5120]{1,0:T(8,128)(2,1)} %copy-done.5, bf16[256,1280]{1,0:T(8,128)(2,1)} %bitcast.107, f32[4,32,128]{2,1,0:T(8,128)} %bitcast.112), custom_call_target="tpu_custom_call" | custom-call | tf_op jit(solution)/shard_map/reduce_mlp/pallas_call | solution.py:868
  448.7 0.7 slice.122
  449.5 0.7 fusion.58
  450.7 7.1 %unpack_attn.1 = (f32[320,3840]{1,0:T(8,128)}, f32[320,1280]{1,0:T(8,128)}) custom-call(bf16[2,4,4,416,128]{4,3,2,1,0:T(8,128)(2,1)} %reduce_attn.1.src), custom_call_target="tpu_custom_call" | custom-call | tf_op jit(solution)/shard_map/unpack_attn/pallas_call | solution.py:1012
  457.9 12.9 %unpack_mlp.1 = (f32[320,5120]{1,0:T(8,128)}, f32[1280,1280]{1,0:T(8,128)}) custom-call(bf16[2,4,4,816,128]{4,3,2,1,0:T(8,128)(2,1)} %reduce_mlp.1.src), custom_call_target="tpu_custom_call" | custom-call | tf_op jit(solution)/shard_map/unpack_mlp/pallas_call | solution.py:983
  (61 shorter events, 4.0 us)
Async XLA Ops:
  9.5 102.0 %copy-start.1 = (bf16[1,256,1280]{2,1,0:T(8,128)(2,1)S(1)}, bf16[1,256,1280]{2,1,0:T(8,128)(2,1)}, u32[]{:S(2)}) copy-start(bf16[1,256,1280]{2,1,0:T(8,128)(2,1)} %param.14) | copy-start | bytes 1966084
  179.5 11.8 %copy-start.4 = (bf16[1,256,1280]{2,1,0:T(8,128)(2,1)S(1)}, bf16[1,256,1280]{2,1,0:T(8,128)(2,1)}, u32[]{:S(2)}) copy-start(bf16[1,256,1280]{2,1,0:T(8,128)(2,1)} %param.15) | copy-start | bytes 1966084
  179.5 11.8 %copy-start.8 = (f32[256,5120]{1,0:T(8,128)S(1)}, f32[256,5120]{1,0:T(8,128)}, u32[]{:S(2)}) copy-start(f32[256,5120]{1,0:T(8,128)} %get-tuple-element.71) | copy-start | bytes 15728644
  199.9 8.7 %copy-start.5 = (bf16[256,5120]{1,0:T(8,128)(2,1)}, bf16[256,5120]{1,0:T(8,128)(2,1)S(1)}, u32[]{:S(2)}) copy-start(bf16[256,5120]{1,0:T(8,128)(2,1)S(1)} %get-tuple-element.73.gp) | copy-start | bytes 7864324
  211.3 3.2 copy-start.7
  214.5 1.1 copy-start.6
  254.9 8.6 %copy-start = (bf16[256,3840]{1,0:T(8,128)(2,1)}, bf16[256,3840]{1,0:T(8,128)(2,1)S(1)}, u32[]{:S(2)}) copy-start(bf16[256,3840]{1,0:T(8,128)(2,1)S(1)} %attention_back.1.gqkv) | copy-start | bytes 5898244
  263.9 3.0 copy-start.2
  264.6 3.7 copy-start.3
